TPU v7x, 128 devices: a whole 4x4x4 slice. The times are simulated.
128 devices in a mesh: tm: 32 (over z, y, x_lo), slab: 4 (over x_hi, core).
Axes of the slice: x: 4 (x_hi: 2, x_lo: 2; x = x_hi * 2 + x_lo), y: 4, z: 4, core: 2. Of those that a mesh axis runs over, the one named last changes fastest.
Arguments:
- kspace: bfloat16 [2, 64, 4, 96, 9984], P(None, 'tm', None, 'slab'), may hold values from -40 to 40, as said below
- sens: float32 [2, 4, 8, 104, 96], P(None, None, None, 'slab'), may hold values from -3 to 3
Outputs:
- projected: float32 [64, 2, 8, 104, 96], P('tm', None, None, 'slab')
Inputs may be any that keep to these rules, and one draw needn't show every extreme that they name: `kspace`: k-space values of order one with frames of different scale.
All inputs are finite; a program needn't handle non-finite values.
Results may differ from a plain program's by a relative error of at most 0.0036.
Values may be sent and summed in bfloat16 or wider, within the bound.
A program may use at most 128 MiB of HBM per device.

v0:
```python
import jax
import jax.numpy as jnp
from jax import lax
from jax.sharding import PartitionSpec as P

NX = 96
NY = 104
NZ = 96
RANK = 32
ITERS = 4
XW = 8


def inverse_table(length, count, offset):
    outputs = jnp.arange(count, dtype=jnp.int32) + offset
    inputs = jnp.arange(length, dtype=jnp.int32)
    phase = outputs[:, None] * inputs[None, :] % length
    angle = phase.astype(jnp.float32) * (2.0 * jnp.pi / length)
    norm_factor = 1.0 / jnp.sqrt(jnp.float32(length))
    return (jnp.cos(angle) * norm_factor, jnp.sin(angle) * norm_factor)


def contract(pattern, matrix_table, operand):
    return jnp.einsum(pattern, matrix_table, operand, precision=lax.Precision.HIGHEST)


def matmul(left, right):
    return jnp.dot(left, right, precision=lax.Precision.HIGHEST)


def orthonormal(rows, gram):
    factor = jnp.linalg.cholesky(matmul(matmul(rows, gram), rows.T))
    return lax.linalg.triangular_solve(factor, rows, left_side=True, lower=True)


def local(kspace, sens):
    frames_dev = kspace.shape[1]
    coil_count = kspace.shape[2]
    depth_dev = kspace.shape[3]
    spectrum = kspace.astype(jnp.float32).reshape(2, frames_dev, coil_count, depth_dev, NX, NY)
    across_cos, across_sin = inverse_table(NX, XW, (NX - XW) // 2)
    down_cos, down_sin = inverse_table(NY, NY, 0)
    depth_cos, depth_sin = inverse_table(NZ, NZ, 0)
    across_real = contract("jx,fczxy->fczjy", across_cos, spectrum[0]) - contract(
        "jx,fczxy->fczjy", across_sin, spectrum[1]
    )
    across_other = contract("jx,fczxy->fczjy", across_cos, spectrum[1]) + contract(
        "jx,fczxy->fczjy", across_sin, spectrum[0]
    )
    down_real = contract("my,fczjy->fczjm", down_cos, across_real) - contract(
        "my,fczjy->fczjm", down_sin, across_other
    )
    down_other = contract("my,fczjy->fczjm", down_cos, across_other) + contract(
        "my,fczjy->fczjm", down_sin, across_real
    )
    planes = jnp.stack([down_real, down_other]).astype(jnp.bfloat16)
    arrived = lax.all_to_all(planes, "slab", split_axis=5, concat_axis=3, tiled=True).astype(
        jnp.float32
    )
    depth_real = contract("wz,fczxy->fcxyw", depth_cos, arrived[0]) - contract(
        "wz,fczxy->fcxyw", depth_sin, arrived[1]
    )
    depth_other = contract("wz,fczxy->fcxyw", depth_cos, arrived[1]) + contract(
        "wz,fczxy->fcxyw", depth_sin, arrived[0]
    )
    sens_real = sens[0][None]
    sens_other = sens[1][None]
    combined_real = jnp.sum(sens_real * depth_real + sens_other * depth_other, axis=1)
    combined_other = jnp.sum(sens_real * depth_other - sens_other * depth_real, axis=1)
    matrix = jnp.stack([combined_real, combined_other], axis=1).reshape(frames_dev, -1)
    rows = lax.all_to_all(matrix, "tm", split_axis=1, concat_axis=0, tiled=True)
    gram = lax.psum(matmul(rows, rows.T), ("tm", "slab"))
    eye = jnp.eye(RANK, dtype=jnp.float32)
    current = jnp.concatenate([eye, eye], axis=1)
    for sweep_index in range(ITERS):
        current = matmul(orthonormal(current, gram), gram)
    coeff = orthonormal(current, gram)
    mixing = matmul(matmul(coeff, gram).T, coeff)
    projected = matmul(mixing, rows)
    projected = lax.all_to_all(projected, "tm", split_axis=0, concat_axis=1, tiled=True)
    return projected.reshape(frames_dev, 2, XW, -1, NZ)


def solution(mesh):
    in_specs = (P(None, "tm", None, "slab", None), P(None, None, None, "slab", None))
    out_specs = P("tm", None, None, "slab", None)
    return jax.shard_map(local, mesh=mesh, in_specs=in_specs, out_specs=out_specs, check_vma=False)
```

profile of v0, /device:TPU:0, one launch (start us, length us, event | category | flops | bytes accessed | tf_op | source)
XLA Modules:
  0.0 234.5 jit_solution(5598859404871233806)
XLA Ops:
  0.0 5.4 %fusion.180 = (bf16[1,2,4,24,9984]{4,3,2,1,0:T(8,128)(2,1)}, bf16[1,2,4,24,9984]{4,3,2,1,0:T(8,128)(2,1)}) fusion(bf16[2,2,4,24,9984]{4,3,2,1,0:T(8,128)(2,1)} %param.5), kind=kLoop, calls=%fused_computation.213 | loop fusion | bytes 15335424 | tf_op jit(solution)/shard_map/slice | solution.py:44
  5.4 13.7 %squeeze.16 = bf16[2,4,24,96,104]{4,3,2,1,0:T(8,128)(2,1)} reshape(bf16[1,2,4,24,9984]{4,3,2,1,0:T(8,128)(2,1)} %get-tuple-element.9) | data formatting | bytes 7667712 | tf_op jit(solution)/shard_map/squeeze | solution.py:44
  19.2 13.8 %squeeze.17 = bf16[2,4,24,96,104]{4,3,2,1,0:T(8,128)(2,1)} reshape(bf16[1,2,4,24,9984]{4,3,2,1,0:T(8,128)(2,1)} %get-tuple-element.10) | data formatting | bytes 7667712 | tf_op jit(solution)/shard_map/squeeze | solution.py:45
  33.0 4.3 %fusion.105 = f32[8,2,4,24,104]{4,0,3,2,1:T(8,128)S(1)} fusion(bf16[2,4,24,96,104]{4,3,2,1,0:T(8,128)(2,1)} %squeeze.16, s32[8]{0:T(128)S(1)} %iota_add_fusion), kind=kOutput, calls=%fused_computation.133 | convolution fusion | flops 184032768 | bytes 4472864 | tf_op jit(solution)/shard_map/jx,fczxy->fczjy/dot_general | solution.py:24
  37.3 2.1 fusion.103
  39.4 2.1 fusion.1
  42.5 2.1 fusion
  48.6 5.8 %copy.42 = bf16[2,2,4,24,8,104]{3,4,2,1,0,5:T(8,128)(2,1)S(1)} copy(bf16[2,2,4,24,8,104]{5,3,4,2,1,0:T(8,128)(2,1)} %pad_maximum_fusion) | data formatting | bytes 1277952 | tf_op jit(solution)/shard_map/stack | solution.py:56
  54.4 5.0 %reshape.64 = bf16[4,2,39936]{2,1,0:T(2,128)(2,1)} reshape(bf16[104,2,2,4,8,24]{5,4,3,2,1,0:T(8,128)(2,1)S(1)} %bitcast.164) | data formatting | bytes 1277952
  59.4 4.4 %all-to-all-start = ((bf16[4,2,39936]{2,1,0:T(2,128)(2,1)}), bf16[4,2,39936]{2,1,0:T(2,128)(2,1)}, u32[]{:S(2)}, u32[]{:S(2)}) async-start(bf16[4,2,39936]{2,1,0:T(2,128)(2,1)} %reshape.64), calls=%async_computation | async-start | bytes 1277952 | tf_op jit(solution)/shard_map/all_to_all | solution.py:57
  66.8 8.7 %all-to-all-done = bf16[4,2,39936]{2,1,0:T(2,128)(2,1)} async-done(((bf16[4,2,39936]{2,1,0:T(2,128)(2,1)}), bf16[4,2,39936]{2,1,0:T(2,128)(2,1)}, u32[]{:S(2)}, u32[]{:S(2)}) %all-to-all-start) | async-done | bytes 639008 | tf_op jit(solution)/shard_map/all_to_all | solution.py:57
  75.5 5.6 %reshape.65 = bf16[104,2,2,4,8,24]{5,4,3,2,1,0:T(8,128)(2,1)S(1)} reshape(bf16[4,2,39936]{2,1,0:T(2,128)(2,1)} %all-to-all-done) | data formatting | bytes 1277952
  81.1 4.4 %copy.86 = bf16[2,2,4,24,8,4,26]{3,5,4,6,2,1,0:T(4,128)(2,1)S(1)} copy(bf16[2,2,4,24,8,4,26]{3,4,2,1,0,6,5:T(8,128)(2,1)S(1)} %bitcast.165) | data formatting | bytes 1277952 | tf_op jit(solution)/shard_map/all_to_all | solution.py:57
  85.5 1.2 fusion.181
  86.7 1.6 squeeze.18
  88.3 2.9 %fusion.16 = f32[2,4,8,26,96]{4,3,2,1,0:T(8,128)} fusion(bf16[2,4,96,8,26]{2,3,4,1,0:T(8,128)(2,1)} %squeeze.18), kind=kOutput, calls=%fused_computation.27 | convolution fusion | flops 184117248 | bytes 958464 | tf_op jit(solution)/shard_map/wz,fczxy->fcxyw/dot_general | solution.py:24
  92.8 2.0 convolution_subtract_fusion
  94.9 2.2 add_reduce_fusion
  98.3 9.4 %all-to-all-start.1 = ((f32[2,32,1248]{2,0,1:T(2,128)}), f32[2,32,1248]{2,0,1:T(2,128)S(1)}, u32[]{:S(2)}, u32[]{:S(2)}) async-start(f32[2,32,1248]{2,0,1:T(2,128)} %copy.49), calls=%async_computation.1 | async-start | bytes 655360 | tf_op jit(solution)/shard_map/all_to_all | solution.py:71
  107.7 9.6 %all-to-all-done.1 = f32[2,32,1248]{2,0,1:T(2,128)S(1)} async-done(((f32[2,32,1248]{2,0,1:T(2,128)}), f32[2,32,1248]{2,0,1:T(2,128)S(1)}, u32[]{:S(2)}, u32[]{:S(2)}) %all-to-all-start.1) | async-done | bytes 319520 | tf_op jit(solution)/shard_map/all_to_all | solution.py:71
  118.2 62.4 %psum.7 = f32[64,64]{1,0:T(8,128)S(1)} all-reduce(f32[64,64]{1,0:T(8,128)S(1)} %fusion.182), channel_id=1, replica_groups=mesh['tm'=32,'slab'=4] {'tm','slab'}, use_global_device_ids=true, to_apply=%region_2.3 | all-reduce | flops 4096 | bytes 32768 | tf_op jit(solution)/shard_map/psum | solution.py:72
  181.1 2.9 %cholesky.89 = f32[32,32]{1,0:T(8,128)S(1)} custom-call(f32[32,32]{1,0:T(8,128)S(1)} %fusion.89), custom_call_target="Cholesky" | custom-call | tf_op jit(solution)/shard_map/jit(cholesky)/cholesky | solution.py:32
  185.4 2.4 %custom-call.9 = f32[1,32,32]{1,2,0:T(8,128)S(1)} custom-call(f32[1,32,32]{2,1,0:T(8,128)S(1)} %fusion.70), custom_call_target="InvertDiagBlocksLowerTriangular" | custom-call | tf_op jit(solution)/shard_map/triangular_solve/custom-call.0 | solution.py:33
  188.6 2.9 %cholesky.100 = f32[32,32]{1,0:T(8,128)S(1)} custom-call(f32[32,32]{1,0:T(8,128)S(1)} %fusion.86), custom_call_target="Cholesky" | custom-call | tf_op jit(solution)/shard_map/jit(cholesky)/cholesky | solution.py:32
  192.9 2.4 %custom-call.10 = f32[1,32,32]{1,2,0:T(8,128)S(1)} custom-call(f32[1,32,32]{2,1,0:T(8,128)S(1)} %fusion.71), custom_call_target="InvertDiagBlocksLowerTriangular" | custom-call | tf_op jit(solution)/shard_map/triangular_solve/custom-call.0 | solution.py:33
  196.1 2.9 %cholesky.111 = f32[32,32]{1,0:T(8,128)S(1)} custom-call(f32[32,32]{1,0:T(8,128)S(1)} %fusion.83), custom_call_target="Cholesky" | custom-call | tf_op jit(solution)/shard_map/jit(cholesky)/cholesky | solution.py:32
  200.4 2.4 %custom-call.11 = f32[1,32,32]{1,2,0:T(8,128)S(1)} custom-call(f32[1,32,32]{2,1,0:T(8,128)S(1)} %fusion.72), custom_call_target="InvertDiagBlocksLowerTriangular" | custom-call | tf_op jit(solution)/shard_map/triangular_solve/custom-call.0 | solution.py:33
  203.6 2.9 %cholesky.122 = f32[32,32]{1,0:T(8,128)S(1)} custom-call(f32[32,32]{1,0:T(8,128)S(1)} %fusion.80), custom_call_target="Cholesky" | custom-call | tf_op jit(solution)/shard_map/jit(cholesky)/cholesky | solution.py:32
  207.8 2.4 %custom-call.12 = f32[1,32,32]{1,2,0:T(8,128)S(1)} custom-call(f32[1,32,32]{2,1,0:T(8,128)S(1)} %fusion.73), custom_call_target="InvertDiagBlocksLowerTriangular" | custom-call | tf_op jit(solution)/shard_map/triangular_solve/custom-call.0 | solution.py:33
  211.1 2.9 %cholesky.133 = f32[32,32]{1,0:T(8,128)S(1)} custom-call(f32[32,32]{1,0:T(8,128)S(1)} %fusion.77), custom_call_target="Cholesky" | custom-call | tf_op jit(solution)/shard_map/jit(cholesky)/cholesky | solution.py:32
  215.3 2.4 %custom-call.13 = f32[1,32,32]{1,2,0:T(8,128)S(1)} custom-call(f32[1,32,32]{2,1,0:T(8,128)S(1)} %fusion.74), custom_call_target="InvertDiagBlocksLowerTriangular" | custom-call | tf_op jit(solution)/shard_map/triangular_solve/custom-call.0 | solution.py:33
  219.1 14.0 %all_to_all.47 = f32[32,2,1248]{2,1,0:T(2,128)S(1)} all-to-all(f32[32,2,1248]{2,1,0:T(2,128)S(1)} %copy.56), channel_id=1, replica_groups=mesh['tm'=32,'slab'=4] {'tm'}, dimensions={0} | all-to-all | bytes 638976 | tf_op jit(solution)/shard_map/all_to_all | solution.py:80
  (80 shorter events, 24.6 us)
Async XLA Ops:
  33.0 4.3 %copy-start = (bf16[2,4,24,96,104]{4,3,2,1,0:T(8,128)(2,1)S(1)}, bf16[2,4,24,96,104]{4,3,2,1,0:T(8,128)(2,1)}, u32[]{:S(2)}) copy-start(bf16[2,4,24,96,104]{4,3,2,1,0:T(8,128)(2,1)} %squeeze.17) | copy-start | bytes 11501572
  37.3 5.1 %slice-start = ((s8[4718592]{0:T(1024)(128)(4,1)}), s8[4194304]{0:T(1024)(128)(4,1)S(1)}, s32[]{:S(2)}) async-start(s8[4718592]{0:T(1024)(128)(4,1)} %bitcast.161), calls=%async_computation.3 | async-start | bytes 8388608
  39.4 3.1 %slice-start.1 = ((s8[4718592]{0:T(1024)(128)(4,1)}), s8[524288]{0:T(1024)(128)(4,1)S(1)}, s32[]{:S(2)}) async-start(s8[4718592]{0:T(1024)(128)(4,1)} %bitcast.161), calls=%async_computation.4 | async-start | bytes 1048576
  59.4 16.1 %all-to-all-start = ((bf16[4,2,39936]{2,1,0:T(2,128)(2,1)}), bf16[4,2,39936]{2,1,0:T(2,128)(2,1)}, u32[]{:S(2)}, u32[]{:S(2)}) async-start(bf16[4,2,39936]{2,1,0:T(2,128)(2,1)} %reshape.64), calls=%async_computation | async-start | bytes 1277952 | tf_op jit(solution)/shard_map/all_to_all | solution.py:57
  88.3 6.6 %copy-start.1 = (bf16[2,4,96,8,26]{2,3,4,1,0:T(8,128)(2,1)S(1)}, bf16[2,4,96,8,26]{2,3,4,1,0:T(8,128)(2,1)}, u32[]{:S(2)}) copy-start(bf16[2,4,96,8,26]{2,3,4,1,0:T(8,128)(2,1)} %squeeze.18) | copy-start | bytes 958468
  88.3 6.6 %copy-start.2 = (f32[4,8,26,96]{3,2,1,0:T(8,128)S(1)}, f32[4,8,26,96]{3,2,1,0:T(8,128)}, u32[]{:S(2)}) copy-start(f32[4,8,26,96]{3,2,1,0:T(8,128)} %copy.37) | copy-start | bytes 958468
  98.3 19.0 %all-to-all-start.1 = ((f32[2,32,1248]{2,0,1:T(2,128)}), f32[2,32,1248]{2,0,1:T(2,128)S(1)}, u32[]{:S(2)}, u32[]{:S(2)}) async-start(f32[2,32,1248]{2,0,1:T(2,128)} %copy.49), calls=%async_computation.1 | async-start | bytes 655360 | tf_op jit(solution)/shard_map/all_to_all | solution.py:71
where the time goes:
time: 235 us; the launch traced here: 234 us
  blocking collectives  76.4 us (33%)
  local copies, waits for them, and re-layouts  64.1 us (27%)
  other arithmetic  34.6 us (15%)
  matrix products  26.8 us (11%)
  waiting for transfers between devices  18.3 us (8%)
  starting transfers between devices  13.7 us (6%)
    psum x1, blocking collectives, local(): gram = lax.psum(matmul(rows, rows.T), ('tm', 'slab'))  62.4 us
    dot_general x12, matrix products, contract(): jnp.einsum(pattern, matrix_table, operand, precision=lax.Precision.HIGHEST)  22.3 us
    another operation x16, other arithmetic, orthonormal(): factor = jnp.linalg.cholesky(matmul(matmul(rows, gram), rows.T))  18 us
    another operation x10, other arithmetic, orthonormal(): return lax.linalg.triangular_solve(factor, rows, left_side=True, lower=True)  15.4 us
    all_to_all x1, blocking collectives, local(): lax.all_to_all(projected, 'tm', split_axis=0, concat_axis=1, tiled=True)  14 us
    squeeze x1, local copies, waits for them, and re-layouts, local(): spectrum[1]  13.8 us
    squeeze x1, local copies, waits for them, and re-layouts, local(): spectrum[0]  13.7 us
    unnamed x12, local copies, waits for them, and re-layouts  10.6 us
  transfers between devices with their start and end apart: 2, of which 2 were waited for; matrix products, arithmetic and copies ran while one was open for 1% of the time, Pallas kernels for 0%

commit v1 on v0

--- a/solution.py
+++ b/solution.py
@@ -9,6 +9,13 @@
 RANK = 32
 ITERS = 4
 XW = 8
+
+
+def exchange_blocks(x, axis, split, join):
+    count = lax.axis_size(axis)
+    blocks = jnp.stack(jnp.split(x, count, axis=split), axis=0)
+    blocks = lax.all_to_all(blocks, axis, split_axis=0, concat_axis=0)
+    return jnp.concatenate(blocks, axis=join)
 
 
 def inverse_table(length, count, offset):
@@ -77,7 +84,7 @@
     coeff = orthonormal(current, gram)
     mixing = matmul(matmul(coeff, gram).T, coeff)
     projected = matmul(mixing, rows)
-    projected = lax.all_to_all(projected, "tm", split_axis=0, concat_axis=1, tiled=True)
+    projected = exchange_blocks(projected, "tm", 0, 1)
     return projected.reshape(frames_dev, 2, XW, -1, NZ)
 
 

time: 235 us -> 235 us (level)
    unnamed x12 -> x43, local copies, waits for them, and re-layouts: 10.6 us -> 11 us
where the time goes in v1:
time: 235 us
  blocking collectives  76.5 us (33%)
  local copies, waits for them, and re-layouts  64 us (27%)
  other arithmetic  34.6 us (15%)
  matrix products  26.8 us (11%)
  waiting for transfers between devices  18.3 us (8%)
  starting transfers between devices  13.7 us (6%)
    psum x1, blocking collectives, local(): gram = lax.psum(matmul(rows, rows.T), ('tm', 'slab'))  62.4 us
    dot_general x12, matrix products, contract(): jnp.einsum(pattern, matrix_table, operand, precision=lax.Precision.HIGHEST)  22.3 us
    another operation x16, other arithmetic, orthonormal(): factor = jnp.linalg.cholesky(matmul(matmul(rows, gram), rows.T))  18 us
    another operation x10, other arithmetic, orthonormal(): return lax.linalg.triangular_solve(factor, rows, left_side=True, lower=True)  15.4 us
    all_to_all x1, blocking collectives, exchange_blocks(): blocks = lax.all_to_all(blocks, axis, split_axis=0, concat_axis=0)  14 us
    squeeze x1, local copies, waits for them, and re-layouts, local(): spectrum[1]  13.8 us
    squeeze x1, local copies, waits for them, and re-layouts, local(): spectrum[0]  13.7 us
    unnamed x43, local copies, waits for them, and re-layouts  11 us
  transfers between devices with their start and end apart: 2, of which 2 were waited for; matrix products, arithmetic and copies ran while one was open for 1% of the time, Pallas kernels for 0%

profile of v1, /device:TPU:0, one launch (start us, length us, event | category | flops | bytes accessed | tf_op | source)
XLA Modules:
  0.0 234.5 jit_solution(14831246014550155394)
XLA Ops:
  0.0 5.4 %fusion.178 = (bf16[1,2,4,24,9984]{4,3,2,1,0:T(8,128)(2,1)}, bf16[1,2,4,24,9984]{4,3,2,1,0:T(8,128)(2,1)}) fusion(bf16[2,2,4,24,9984]{4,3,2,1,0:T(8,128)(2,1)} %param.5), kind=kLoop, calls=%fused_computation.275 | loop fusion | bytes 15335424 | tf_op jit(solution)/shard_map/slice | solution.py:51
  5.4 13.7 %squeeze.16 = bf16[2,4,24,96,104]{4,3,2,1,0:T(8,128)(2,1)} reshape(bf16[1,2,4,24,9984]{4,3,2,1,0:T(8,128)(2,1)} %get-tuple-element.9) | data formatting | bytes 7667712 | tf_op jit(solution)/shard_map/squeeze | solution.py:51
  19.2 13.8 %squeeze.17 = bf16[2,4,24,96,104]{4,3,2,1,0:T(8,128)(2,1)} reshape(bf16[1,2,4,24,9984]{4,3,2,1,0:T(8,128)(2,1)} %get-tuple-element.10) | data formatting | bytes 7667712 | tf_op jit(solution)/shard_map/squeeze | solution.py:52
  33.0 4.3 %fusion.103 = f32[8,2,4,24,104]{4,0,3,2,1:T(8,128)S(1)} fusion(bf16[2,4,24,96,104]{4,3,2,1,0:T(8,128)(2,1)} %squeeze.16, s32[8]{0:T(128)S(1)} %iota_add_fusion), kind=kOutput, calls=%fused_computation.195 | convolution fusion | flops 184032768 | bytes 4472864 | tf_op jit(solution)/shard_map/jx,fczxy->fczjy/dot_general | solution.py:31
  37.3 2.1 fusion.101
  39.4 2.1 fusion.1
  42.5 2.1 fusion
  48.6 5.8 %copy.40 = bf16[2,2,4,24,8,104]{3,4,2,1,0,5:T(8,128)(2,1)S(1)} copy(bf16[2,2,4,24,8,104]{5,3,4,2,1,0:T(8,128)(2,1)} %pad_maximum_fusion) | data formatting | bytes 1277952 | tf_op jit(solution)/shard_map/stack | solution.py:63
  54.4 5.0 %reshape.57 = bf16[4,2,39936]{2,1,0:T(2,128)(2,1)} reshape(bf16[104,2,2,4,8,24]{5,4,3,2,1,0:T(8,128)(2,1)S(1)} %bitcast.292) | data formatting | bytes 1277952
  59.4 4.4 %all-to-all-start = ((bf16[4,2,39936]{2,1,0:T(2,128)(2,1)}), bf16[4,2,39936]{2,1,0:T(2,128)(2,1)}, u32[]{:S(2)}, u32[]{:S(2)}) async-start(bf16[4,2,39936]{2,1,0:T(2,128)(2,1)} %reshape.57), calls=%async_computation | async-start | bytes 1277952 | tf_op jit(solution)/shard_map/all_to_all | solution.py:64
  66.8 8.7 %all-to-all-done = bf16[4,2,39936]{2,1,0:T(2,128)(2,1)} async-done(((bf16[4,2,39936]{2,1,0:T(2,128)(2,1)}), bf16[4,2,39936]{2,1,0:T(2,128)(2,1)}, u32[]{:S(2)}, u32[]{:S(2)}) %all-to-all-start) | async-done | bytes 639008 | tf_op jit(solution)/shard_map/all_to_all | solution.py:64
  75.5 5.6 %reshape.58 = bf16[104,2,2,4,8,24]{5,4,3,2,1,0:T(8,128)(2,1)S(1)} reshape(bf16[4,2,39936]{2,1,0:T(2,128)(2,1)} %all-to-all-done) | data formatting | bytes 1277952
  81.1 4.4 %copy.80 = bf16[2,2,4,24,8,4,26]{3,5,4,6,2,1,0:T(4,128)(2,1)S(1)} copy(bf16[2,2,4,24,8,4,26]{3,4,2,1,0,6,5:T(8,128)(2,1)S(1)} %bitcast.293) | data formatting | bytes 1277952 | tf_op jit(solution)/shard_map/all_to_all | solution.py:64
  85.5 1.2 fusion.179
  86.7 1.6 squeeze.18
  88.3 2.9 %fusion.16 = f32[2,4,8,26,96]{4,3,2,1,0:T(8,128)} fusion(bf16[2,4,96,8,26]{2,3,4,1,0:T(8,128)(2,1)} %squeeze.18), kind=kOutput, calls=%fused_computation.27 | convolution fusion | flops 184117248 | bytes 958464 | tf_op jit(solution)/shard_map/wz,fczxy->fcxyw/dot_general | solution.py:31
  92.8 2.0 convolution_subtract_fusion
  94.9 2.2 add_reduce_fusion
  98.3 9.4 %all-to-all-start.1 = ((f32[2,32,1248]{2,0,1:T(2,128)}), f32[2,32,1248]{2,0,1:T(2,128)S(1)}, u32[]{:S(2)}, u32[]{:S(2)}) async-start(f32[2,32,1248]{2,0,1:T(2,128)} %copy.47), calls=%async_computation.1 | async-start | bytes 655360 | tf_op jit(solution)/shard_map/all_to_all | solution.py:78
  107.7 9.6 %all-to-all-done.1 = f32[2,32,1248]{2,0,1:T(2,128)S(1)} async-done(((f32[2,32,1248]{2,0,1:T(2,128)}), f32[2,32,1248]{2,0,1:T(2,128)S(1)}, u32[]{:S(2)}, u32[]{:S(2)}) %all-to-all-start.1) | async-done | bytes 319520 | tf_op jit(solution)/shard_map/all_to_all | solution.py:78
  117.9 62.4 %psum.7 = f32[64,64]{1,0:T(8,128)S(1)} all-reduce(f32[64,64]{1,0:T(8,128)S(1)} %fusion.180), channel_id=1, replica_groups=mesh['tm'=32,'slab'=4] {'tm','slab'}, use_global_device_ids=true, to_apply=%region_2.3 | all-reduce | flops 4096 | bytes 32768 | tf_op jit(solution)/shard_map/psum | solution.py:79
  180.9 2.9 %cholesky.89 = f32[32,32]{1,0:T(8,128)S(1)} custom-call(f32[32,32]{1,0:T(8,128)S(1)} %fusion.87), custom_call_target="Cholesky" | custom-call | tf_op jit(solution)/shard_map/jit(cholesky)/cholesky | solution.py:39
  185.1 2.4 %custom-call.9 = f32[1,32,32]{1,2,0:T(8,128)S(1)} custom-call(f32[1,32,32]{2,1,0:T(8,128)S(1)} %fusion.68), custom_call_target="InvertDiagBlocksLowerTriangular" | custom-call | tf_op jit(solution)/shard_map/triangular_solve/custom-call.0 | solution.py:40
  188.4 2.9 %cholesky.100 = f32[32,32]{1,0:T(8,128)S(1)} custom-call(f32[32,32]{1,0:T(8,128)S(1)} %fusion.84), custom_call_target="Cholesky" | custom-call | tf_op jit(solution)/shard_map/jit(cholesky)/cholesky | solution.py:39
  192.6 2.4 %custom-call.10 = f32[1,32,32]{1,2,0:T(8,128)S(1)} custom-call(f32[1,32,32]{2,1,0:T(8,128)S(1)} %fusion.69), custom_call_target="InvertDiagBlocksLowerTriangular" | custom-call | tf_op jit(solution)/shard_map/triangular_solve/custom-call.0 | solution.py:40
  195.9 2.9 %cholesky.111 = f32[32,32]{1,0:T(8,128)S(1)} custom-call(f32[32,32]{1,0:T(8,128)S(1)} %fusion.81), custom_call_target="Cholesky" | custom-call | tf_op jit(solution)/shard_map/jit(cholesky)/cholesky | solution.py:39
  200.1 2.4 %custom-call.11 = f32[1,32,32]{1,2,0:T(8,128)S(1)} custom-call(f32[1,32,32]{2,1,0:T(8,128)S(1)} %fusion.70), custom_call_target="InvertDiagBlocksLowerTriangular" | custom-call | tf_op jit(solution)/shard_map/triangular_solve/custom-call.0 | solution.py:40
  203.4 2.9 %cholesky.122 = f32[32,32]{1,0:T(8,128)S(1)} custom-call(f32[32,32]{1,0:T(8,128)S(1)} %fusion.78), custom_call_target="Cholesky" | custom-call | tf_op jit(solution)/shard_map/jit(cholesky)/cholesky | solution.py:39
  207.6 2.4 %custom-call.12 = f32[1,32,32]{1,2,0:T(8,128)S(1)} custom-call(f32[1,32,32]{2,1,0:T(8,128)S(1)} %fusion.71), custom_call_target="InvertDiagBlocksLowerTriangular" | custom-call | tf_op jit(solution)/shard_map/triangular_solve/custom-call.0 | solution.py:40
  210.8 2.9 %cholesky.133 = f32[32,32]{1,0:T(8,128)S(1)} custom-call(f32[32,32]{1,0:T(8,128)S(1)} %fusion.75), custom_call_target="Cholesky" | custom-call | tf_op jit(solution)/shard_map/jit(cholesky)/cholesky | solution.py:39
  215.1 2.4 %custom-call.13 = f32[1,32,32]{1,2,0:T(8,128)S(1)} custom-call(f32[1,32,32]{2,1,0:T(8,128)S(1)} %fusion.72), custom_call_target="InvertDiagBlocksLowerTriangular" | custom-call | tf_op jit(solution)/shard_map/triangular_solve/custom-call.0 | solution.py:40
  219.2 14.0 %all_to_all.39 = f32[32,2,1248]{2,1,0:T(2,128)S(1)} all-to-all(f32[32,2,1248]{2,1,0:T(2,128)S(1)} %constant_dynamic-update-slice_fusion), channel_id=1, replica_groups=mesh['tm'=32,'slab'=4] {'tm'}, dimensions={0} | all-to-all | bytes 638976 | tf_op jit(solution)/shard_map/all_to_all | solution.py:17
  (110 shorter events, 24.5 us)
Async XLA Ops:
  33.0 4.3 %copy-start = (bf16[2,4,24,96,104]{4,3,2,1,0:T(8,128)(2,1)S(1)}, bf16[2,4,24,96,104]{4,3,2,1,0:T(8,128)(2,1)}, u32[]{:S(2)}) copy-start(bf16[2,4,24,96,104]{4,3,2,1,0:T(8,128)(2,1)} %squeeze.17) | copy-start | bytes 11501572
  37.3 5.1 %slice-start = ((s8[4718592]{0:T(1024)(128)(4,1)}), s8[4194304]{0:T(1024)(128)(4,1)S(1)}, s32[]{:S(2)}) async-start(s8[4718592]{0:T(1024)(128)(4,1)} %bitcast.289), calls=%async_computation.3 | async-start | bytes 8388608
  39.4 3.1 %slice-start.1 = ((s8[4718592]{0:T(1024)(128)(4,1)}), s8[524288]{0:T(1024)(128)(4,1)S(1)}, s32[]{:S(2)}) async-start(s8[4718592]{0:T(1024)(128)(4,1)} %bitcast.289), calls=%async_computation.4 | async-start | bytes 1048576
  59.4 16.1 %all-to-all-start = ((bf16[4,2,39936]{2,1,0:T(2,128)(2,1)}), bf16[4,2,39936]{2,1,0:T(2,128)(2,1)}, u32[]{:S(2)}, u32[]{:S(2)}) async-start(bf16[4,2,39936]{2,1,0:T(2,128)(2,1)} %reshape.57), calls=%async_computation | async-start | bytes 1277952 | tf_op jit(solution)/shard_map/all_to_all | solution.py:64
  88.3 6.6 %copy-start.1 = (bf16[2,4,96,8,26]{2,3,4,1,0:T(8,128)(2,1)S(1)}, bf16[2,4,96,8,26]{2,3,4,1,0:T(8,128)(2,1)}, u32[]{:S(2)}) copy-start(bf16[2,4,96,8,26]{2,3,4,1,0:T(8,128)(2,1)} %squeeze.18) | copy-start | bytes 958468
  88.3 6.6 %copy-start.2 = (f32[4,8,26,96]{3,2,1,0:T(8,128)S(1)}, f32[4,8,26,96]{3,2,1,0:T(8,128)}, u32[]{:S(2)}) copy-start(f32[4,8,26,96]{3,2,1,0:T(8,128)} %copy.35) | copy-start | bytes 958468
  98.3 19.0 %all-to-all-start.1 = ((f32[2,32,1248]{2,0,1:T(2,128)}), f32[2,32,1248]{2,0,1:T(2,128)S(1)}, u32[]{:S(2)}, u32[]{:S(2)}) async-start(f32[2,32,1248]{2,0,1:T(2,128)} %copy.47), calls=%async_computation.1 | async-start | bytes 655360 | tf_op jit(solution)/shard_map/all_to_all | solution.py:78
